TPU v7x, 32 devices: a whole 2x2x4 slice. The times are simulated.
32 devices in a mesh: groups: 2 (over y), seq: 4 (over z), phase: 4 (over x, core).
Axes of the slice: x: 2, y: 2, z: 4, core: 2. Of those that a mesh axis runs over, the one named last changes fastest.
Arguments:
- phase_rows: bfloat16 [4, 512, 3072], P('phase', ('groups', 'seq')), parts along dimension 1, may hold values from -6 to 6
- fresh_rows: bfloat16 [512, 3072], P(('groups', 'seq')), parts along dimension 0, may hold values from -6 to 6
- token_counts: int32 [10], P('groups'), parts along dimension 0, may hold values from 2 to 256, as said below
- memory: float32 [4, 384, 3072], P('phase', 'groups', 'seq'), parts along dimension 1, may hold values from -24 to 24
- normalizer: float32 [4, 384], P('phase', 'groups'), parts along dimension 1, may hold values from 0.05 to 0.5
- w_memq: bfloat16 [4, 3072, 32], P('phase'), may hold values from -0.109375 to 0.109375
- w_memk: bfloat16 [4, 3072, 32], P('phase'), may hold values from -0.109375 to 0.109375
- norm_gain: float32 [4, 3072], P('phase'), may hold values from 0.5 to 1.5
- w_kv: bfloat16 [4, 3072, 1024], P('phase', 'seq'), may hold values from -2 to 2
- w_out: bfloat16 [4, 512, 3072], P('phase', 'seq'), may hold values from -0.25 to 0.25
Outputs:
- rows_out: bfloat16 [4, 512, 3072], P('phase', ('groups', 'seq')), parts along dimension 1
- memory_out: float32 [4, 384, 3072], P('phase', 'groups', 'seq'), parts along dimension 1
- normalizer_out: float32 [4, 384], P('phase', 'groups'), parts along dimension 1
There are 2 independent parts, one for each index of `groups`. A program takes and returns all parts, laid end to end along the dimension named above; an argument that names none is the same for every part. Nothing has to cross between parts.
Inputs may be any that keep to these rules, and one draw needn't show every extreme that they name: token_counts[0] counts the valid tokens of the segment entering section 0 in the second step and token_counts[s + 1] those of the segment at section s in the first step; valid tokens are the first ones of a segment; at least one entry equals 256.
All inputs are finite; a program needn't handle non-finite values.
Results may differ from a plain program's by a relative error of at most 0.024.
Values may be sent and summed in bfloat16 or wider, within the bound.
A program may use at most 64 MiB of HBM per device.

v0:
```python
import math

import jax
import jax.numpy as jnp
from jax import lax
from jax.sharding import PartitionSpec as P

HEAD_DIM = 128


PRECISE = lax.Precision.HIGHEST


def from_behind(value, axis, steps):
    count = lax.axis_size(axis)
    first, last = (max(0, -steps), min(count, count - steps))
    return lax.ppermute(value, axis, [(source, source + steps) for source in range(first, last)])


def features(projected):
    halves = jnp.concatenate([jax.nn.relu(projected), jax.nn.relu(-projected)], axis=-1)
    return jnp.concatenate(
        [halves * jnp.roll(halves, offset, axis=-1) for offset in (1, 2, 3)], axis=-1
    )


def recall(feature_rows, memory_state, norm_state):
    numerator = jnp.dot(feature_rows, memory_state, precision=PRECISE)
    denominator = jnp.dot(feature_rows, norm_state, precision=PRECISE) + 1.0
    return numerator / denominator[:, None]


def attend(keyval, valid_count, position, head_count):
    token_rows = keyval.shape[0]
    kv_width = head_count * HEAD_DIM
    queries = keyval[:, :kv_width].reshape(token_rows, head_count, HEAD_DIM)
    divisor = math.sqrt(HEAD_DIM)

    def absorb_block(running, block_rows, first_row):
        highest, summed, weighted = running
        piece_rows = block_rows.shape[0]
        piece_keys = block_rows[:, :kv_width].reshape(piece_rows, head_count, HEAD_DIM)
        piece_values = (
            block_rows[:, kv_width:].reshape(piece_rows, head_count, HEAD_DIM).astype(jnp.float32)
        )
        scores = (
            jnp.einsum("qhd,khd->hqk", queries, piece_keys, preferred_element_type=jnp.float32)
            / divisor
        )
        key_position = first_row + jnp.arange(piece_rows)
        allowed = (key_position[None, :] < valid_count) & (
            key_position[None, :] != position[:, None]
        )
        masked = jnp.where(allowed[None], scores, -1e30)
        new_highest = jnp.maximum(highest, jnp.max(masked, axis=-1))
        weights = jnp.where(allowed[None], jnp.exp(masked - new_highest[..., None]), 0.0)
        shrink = jnp.exp(highest - new_highest)
        summed = summed * shrink + jnp.sum(weights, axis=-1)
        weighted = weighted * shrink[..., None] + jnp.einsum(
            "hqk,khd->hqd", weights, piece_values, precision=PRECISE
        )
        return (new_highest, summed, weighted)

    initial = (
        jnp.full((head_count, token_rows), -1e30, jnp.float32),
        jnp.zeros((head_count, token_rows), jnp.float32),
        jnp.zeros((head_count, token_rows, HEAD_DIM), jnp.float32),
    )
    running = initial
    shard_rows = lax.all_gather(keyval, "seq", axis=0, tiled=True)
    piece_rows = shard_rows.shape[0]
    block = piece_rows
    while block > 1024 and block % 2 == 0:
        block = block // 2
    block_count = piece_rows // block
    blocks = shard_rows.reshape(block_count, block, shard_rows.shape[1])
    starts = block * jnp.arange(block_count, dtype=jnp.int32)

    def one_block(carry, item):
        block_rows, block_start = item
        return (absorb_block(carry, block_rows, block_start), None)

    running, unused = lax.scan(one_block, running, (blocks, starts))
    highest, summed, weighted = running
    attended = weighted / summed[..., None]
    return jnp.transpose(attended, (1, 0, 2)).reshape(token_rows, kv_width).astype(jnp.bfloat16)


def run_section(in_rows, valid_count, reader, position, params):
    w_memq, w_memk, norm_gain, weights_full, out_full = params
    head_count = out_full.shape[0] // HEAD_DIM
    query_features = features(jnp.dot(in_rows, w_memq, preferred_element_type=jnp.float32))
    residual = in_rows.astype(jnp.float32) + reader(query_features)
    inverse_rms = lax.rsqrt(jnp.mean(residual * residual, axis=-1, keepdims=True) + 1e-05)
    normed = (residual * inverse_rms * norm_gain).astype(jnp.bfloat16)
    keyval = jnp.dot(normed, weights_full, preferred_element_type=jnp.float32).astype(jnp.bfloat16)
    attended = attend(keyval, valid_count, position, head_count)
    output = (residual + jnp.dot(attended, out_full, preferred_element_type=jnp.float32)).astype(
        jnp.bfloat16
    )
    key_features = features(jnp.dot(output, w_memk, preferred_element_type=jnp.float32))
    live_rows = (position < valid_count).astype(jnp.float32)[:, None]
    correction = (output.astype(jnp.float32) - reader(key_features)) * live_rows
    key_features = key_features * live_rows
    update = lax.dot_general(key_features, correction, (((0,), (0,)), ((), ())), precision=PRECISE)
    return (output, update, jnp.sum(key_features, axis=0))


def per_device(
    phase_rows, fresh_rows, token_counts, memory, normalizer, w_memq, w_memk, norm_gain, w_kv, w_out
):
    token_rows = phase_rows.shape[1]
    section_index = lax.axis_index("phase")
    seq_index = lax.axis_index("seq")
    position = seq_index * token_rows + jnp.arange(token_rows)
    weights_full, out_full = (
        lax.all_gather(w_kv[0], "seq", axis=0, tiled=True),
        lax.all_gather(w_out[0], "seq", axis=0, tiled=True),
    )
    memory_cols = memory[0]
    column_width = memory_cols.shape[1]
    memory_full = lax.all_gather(memory_cols, "seq", axis=1, tiled=True)
    norm_now = normalizer[0]
    params = (w_memq[0], w_memk[0], norm_gain[0], weights_full, out_full)

    def first_reader(feature_rows):
        return recall(feature_rows, memory_full, norm_now)

    first_rows, first_update, first_counts = run_section(
        phase_rows[0], token_counts[section_index + 1], first_reader, position, params
    )
    summed, counted = (
        lax.psum(first_update.astype(jnp.bfloat16), "seq").astype(jnp.float32),
        lax.psum(first_counts.astype(jnp.bfloat16), "seq").astype(jnp.float32),
    )
    later_full = memory_full + summed
    later_norm = norm_now + counted
    later_cols = lax.dynamic_slice_in_dim(later_full, seq_index * column_width, column_width, 1)

    def later_reader(feature_rows):
        return recall(feature_rows, later_full, later_norm)

    incoming = from_behind(first_rows, "phase", 1)
    second_in = jnp.where(section_index == 0, fresh_rows, incoming)
    second_rows, second_update, second_counts = run_section(
        second_in, token_counts[section_index], later_reader, position, params
    )
    final_share = lax.psum_scatter(
        second_update.astype(jnp.bfloat16), "seq", scatter_dimension=1, tiled=True
    ).astype(jnp.float32)
    final_counts = lax.psum(second_counts.astype(jnp.bfloat16), "seq").astype(jnp.float32)
    return (second_rows[None], (later_cols + final_share)[None], (later_norm + final_counts)[None])


def solution(mesh):
    return jax.shard_map(
        per_device,
        mesh=mesh,
        in_specs=(
            P("phase", ("groups", "seq"), None),
            P(("groups", "seq"), None),
            P("groups"),
            P("phase", "groups", "seq"),
            P("phase", "groups"),
            P("phase", None, None),
            P("phase", None, None),
            P("phase", None),
            P("phase", "seq", None),
            P("phase", "seq", None),
        ),
        out_specs=(
            P("phase", ("groups", "seq"), None),
            P("phase", "groups", "seq"),
            P("phase", "groups"),
        ),
        check_vma=False,
    )
```

profile of v0, /device:TPU:0, one launch (start us, length us, event | category | flops | bytes accessed | tf_op | source)
XLA Modules:
  0.0 384.0 jit_solution(1830468465455954821)
XLA Ops:
  10.4 1.2 compare_convert_fusion.1
  12.7 1.3 iota_compare_fusion.1
  14.4 48.4 %all-gather.7.cloned.1.call-done = f32[1,192,3072]{2,1,0:T(8,128)} async-done(((f32[1,192,768]{2,1,0:T(8,128)}), f32[1,192,3072]{2,1,0:T(8,128)}) %all-gather.7.cloned.1.call-update) | async-done | bytes 2359312 | tf_op jit(solution)/shard_map/all_gather | solution.py:122
  62.8 3.4 multiply_reduce_fusion.1
  66.2 112.4 %all-gather.9.cloned.1.call-done = bf16[1,3072,1024]{2,1,0:T(8,128)(2,1)} async-done(((bf16[1,768,1024]{2,1,0:T(8,128)(2,1)}), bf16[1,3072,1024]{2,1,0:T(8,128)(2,1)}) %all-gather.9.cloned.1.call-update) | async-done | bytes 6291472 | tf_op jit(solution)/shard_map/all_gather | solution.py:117
  178.6 4.0 %fusion.17 = bf16[64,1024]{1,0:T(8,128)(2,1)S(1)} fusion(bf16[1,3072,1024]{2,1,0:T(8,128)(2,1)} %all-gather.9.cloned.1.call-done, f32[64,3072]{1,0:T(8,128)S(1)} %get-tuple-element.84, f32[3072]{0:T(1024)S(1)} %bitcast.171, f32[64]{0:T(128)S(1)} %add_rsqrt_fusion.1), kind=kOutput, calls=%fused_computation.28 | convolution fusion | flops 403308544 | bytes 7221504 | tf_op jit(solution)/shard_map/dot_general | solution.py:96
  182.6 19.3 %all_gather.17 = bf16[256,1024]{1,0:T(8,128)(2,1)S(1)} all-gather(bf16[64,1024]{1,0:T(8,128)(2,1)S(1)} %fusion.17), channel_id=1, replica_groups=mesh['groups'=2,'seq'=4,'phase'=4] {'seq'}, dimensions={0}, use_global_device_ids=true | all-gather | bytes 655360 | tf_op jit(solution)/shard_map/all_gather | solution.py:70
  203.5 43.5 %all-gather.11.cloned.1.call-done = bf16[1,512,3072]{2,1,0:T(8,128)(2,1)} async-done(((bf16[1,128,3072]{2,1,0:T(8,128)(2,1)}), bf16[1,512,3072]{2,1,0:T(8,128)(2,1)}) %all-gather.11.cloned.1.call-update) | async-done | bytes 3145744 | tf_op jit(solution)/shard_map/all_gather | solution.py:118
  247.0 3.3 fusion.9
  250.4 1.2 negate_maximum_fusion.1
  251.7 2.7 collective-permute-start
  254.6 2.6 fusion.7
  257.3 3.0 convolution_convert_fusion.1
  260.5 9.4 %psum.22 = bf16[192]{0:T(256)(128)(2,1)S(1)} all-reduce(bf16[192]{0:T(256)(128)(2,1)S(1)} %multiply_reduce_fusion.3), channel_id=1, replica_groups=mesh['groups'=2,'seq'=4,'phase'=4] {'seq'}, use_global_device_ids=true, to_apply=%region_5.6 | all-reduce | flops 192 | bytes 768 | tf_op jit(solution)/shard_map/psum | solution.py:134
  270.5 44.2 %all-reduce.2.cloned.1.call-done = bf16[192,3072]{1,0:T(8,128)(2,1)} async-done(((bf16[192,3072]{1,0:T(8,128)(2,1)}), bf16[192,3072]{1,0:T(8,128)(2,1)}) %all-reduce.2.cloned.1.call-update) | async-done | bytes 1179664 | tf_op jit(solution)/shard_map/psum | solution.py:133
  314.7 1.5 bitcast_add_fusion
  316.2 1.8 multiply_reduce_fusion
  318.0 4.1 %fusion.20 = bf16[64,1024]{1,0:T(8,128)(2,1)S(1)} fusion(bf16[1,3072,1024]{2,1,0:T(8,128)(2,1)} %all-gather.9.cloned.1.call-done, f32[64,3072]{1,0:T(8,128)S(1)} %get-tuple-element.88, f32[64]{0:T(128)S(1)} %add_rsqrt_fusion, f32[3072]{0:T(1024)S(1)} %bitcast.172), kind=kOutput, calls=%fused_computation.29 | convolution fusion | flops 403308544 | bytes 7221504 | tf_op jit(solution)/shard_map/dot_general | solution.py:96
  322.1 16.3 %all_gather.19 = bf16[256,1024]{1,0:T(8,128)(2,1)S(1)} all-gather(bf16[64,1024]{1,0:T(8,128)(2,1)S(1)} %fusion.20), channel_id=1, replica_groups=mesh['groups'=2,'seq'=4,'phase'=4] {'seq'}, dimensions={0}, use_global_device_ids=true | all-gather | bytes 655360 | tf_op jit(solution)/shard_map/all_gather | solution.py:70
  340.7 1.6 fusion.5
  342.3 3.0 convolution_convert_fusion
  345.5 10.6 %psum.23 = bf16[192]{0:T(256)(128)(2,1)S(1)} all-reduce(bf16[192]{0:T(256)(128)(2,1)S(1)} %multiply_reduce_fusion.2), channel_id=1, replica_groups=mesh['groups'=2,'seq'=4,'phase'=4] {'seq'}, use_global_device_ids=true, to_apply=%region_11.12 | all-reduce | flops 192 | bytes 768 | tf_op jit(solution)/shard_map/psum | solution.py:151
  356.7 18.7 %reduce-scatter.2.cloned.1.call-done = bf16[192,768]{1,0:T(8,128)(2,1)} async-done(((bf16[192,3072]{1,0:T(8,128)(2,1)}), bf16[192,768]{1,0:T(8,128)(2,1)}) %reduce-scatter.2.cloned.1.call-update) | async-done | bytes 294928 | tf_op jit(solution)/shard_map/reduce_scatter | solution.py:148
  375.5 2.0 add_bitcast_fusion
  (103 shorter events, 9.8 us)
Async XLA Ops:
  7.2 2.3 copy-start
  7.2 2.3 copy-start.5
  7.2 2.6 copy-start.12
  7.2 6.9 %copy-start.13 = (f32[1,192]{1,0:T(1,128)S(1)}, f32[1,192]{1,0:T(1,128)}, u32[]{:S(2)}) copy-start(f32[1,192]{1,0:T(1,128)} %param.14) | copy-start | bytes 2308
  7.2 55.6 %all-gather.7.cloned.1.call-start = ((), (), s32[]{:S(2)}) async-start(), calls=%async_computation.3 | async-start | bytes 2949120 | tf_op jit(solution)/shard_map/all_gather | solution.py:122
  7.9 170.7 %all-gather.9.cloned.1.call-start = ((), (), s32[]{:S(2)}) async-start(), calls=%async_computation.4 | async-start | bytes 7864320 | tf_op jit(solution)/shard_map/all_gather | solution.py:117
  8.7 238.3 %all-gather.11.cloned.1.call-start = ((), (), s32[]{:S(2)}) async-start(), calls=%async_computation.5 | async-start | bytes 3932160 | tf_op jit(solution)/shard_map/all_gather | solution.py:118
  9.4 169.2 %copy-start.7 = (f32[1,3072]{1,0:T(1,128)S(1)}, f32[1,3072]{1,0:T(1,128)}, u32[]{:S(2)}) copy-start(f32[1,3072]{1,0:T(1,128)} %param.17) | copy-start | bytes 36868
  9.4 305.2 %all-reduce.2.cloned.1.call-start = ((), (), s32[]{:S(2)}) async-start(), calls=%async_computation.1 | async-start | bytes 2359296 | tf_op jit(solution)/shard_map/psum | solution.py:133
  203.5 46.9 %copy-start.6 = (bf16[1,3072,32]{1,2,0:T(8,128)(2,1)S(1)}, bf16[1,3072,32]{1,2,0:T(8,128)(2,1)}, u32[]{:S(2)}) copy-start(bf16[1,3072,32]{1,2,0:T(8,128)(2,1)} %param.16) | copy-start | bytes 589828
  203.5 51.0 %copy-start.1 = (f32[1,192,3072]{2,1,0:T(8,128)S(1)}, f32[1,192,3072]{2,1,0:T(8,128)}, u32[]{:S(2)}) copy-start(f32[1,192,3072]{2,1,0:T(8,128)} %all-gather.7.cloned.1.call-done) | copy-start | bytes 7077892
  247.0 7.4 %copy-start.14 = (f32[1,192]{1,0:T(1,128)S(1)}, f32[1,192]{1,0:T(1,128)}, u32[]{:S(2)}) copy-start(f32[1,192]{1,0:T(1,128)} %param.14) | copy-start | bytes 2308
  247.0 7.5 %copy-start.10 = (f32[64]{0:T(128)S(1)}, f32[64]{0:T(128)}, u32[]{:S(2)}) copy-start(f32[64]{0:T(128)} %compare_convert_fusion.1) | copy-start | bytes 772
  251.7 18.2 %collective-permute-start = (bf16[64,3072]{1,0:T(8,128)(2,1)}, bf16[64,3072]{1,0:T(8,128)(2,1)}, u32[]{:S(2)}, u32[]{:S(2)}) collective-permute-start(bf16[64,3072]{1,0:T(8,128)(2,1)} %fusion.9), channel_id=1, source_target_pairs={{0,1},{1,2},{2,3},{4,5},{5,6},{6,7},{8,9},{9,10},{10,11},{12,13},{... | collective-permute-start | bytes 1179656 | tf_op jit(solution)/shard_map/ppermute | solution.py:17
  257.2 3.1 copy-start.11
  257.2 12.7 %copy-start.15 = (f32[1,192]{1,0:T(1,128)S(1)}, f32[1,192]{1,0:T(1,128)}, u32[]{:S(2)}) copy-start(f32[1,192]{1,0:T(1,128)} %param.14) | copy-start | bytes 2308
  257.3 12.7 %copy-start.16 = (bf16[64,3072]{1,0:T(8,128)(2,1)S(1)}, bf16[64,3072]{1,0:T(8,128)(2,1)}, u32[]{:S(2)}) copy-start(bf16[64,3072]{1,0:T(8,128)(2,1)} %param.11) | copy-start | bytes 1179652
  260.3 115.1 %reduce-scatter.2.cloned.1.call-start = ((), (), s32[]{:S(2)}) async-start(), calls=%async_computation.2 | async-start | bytes 1474560 | tf_op jit(solution)/shard_map/reduce_scatter | solution.py:148
  316.2 24.5 %copy-start.3 = (f32[192,3072]{1,0:T(8,128)}, f32[192,3072]{1,0:T(8,128)S(1)}, u32[]{:S(2)}) copy-start(f32[192,3072]{1,0:T(8,128)S(1)} %bitcast_add_fusion) | copy-start | bytes 7077892
  316.2 1.8 copy-start.8
  322.1 17.3 %copy-start.2 = (bf16[1,512,3072]{2,1,0:T(8,128)(2,1)S(1)}, bf16[1,512,3072]{2,1,0:T(8,128)(2,1)}, u32[]{:S(2)}) copy-start(bf16[1,512,3072]{2,1,0:T(8,128)(2,1)} %all-gather.11.cloned.1.call-done) | copy-start | bytes 9437188
  339.4 1.3 copy-start.9
  340.1 2.2 copy-start.4
Sparse Core Ops, SparseCore 0:
  9.6 53.1 all-gather.6
  64.4 114.1 all-gather.8
  180.2 66.7 all-gather.10
  260.4 54.1 all-reduce.1
  345.5 29.8 reduce-scatter.1
where the time goes:
time: 385 us; the launch traced here: 384 us
  waiting for transfers between devices  269 us (70%)
  blocking collectives  55.7 us (14%)
  matrix products  32.3 us (8%)
  between operations  14.4 us (4%)
  other arithmetic  8.66 us (2%)
    all_gather x1, waiting for transfers between devices, per_device(): lax.all_gather(w_kv[0], 'seq', axis=0, tiled=True)  112 us
    all_gather x1, waiting for transfers between devices, per_device(): memory_full = lax.all_gather(memory_cols, 'seq', axis=1, tiled=True)  48.4 us
    psum x1, waiting for transfers between devices, per_device(): lax.psum(first_update.astype(jnp.bfloat16), 'seq').astype(jnp.float32)  44.2 us
    all_gather x1, waiting for transfers between devices, per_device(): lax.all_gather(w_out[0], 'seq', axis=0, tiled=True)  43.5 us
    all_gather x2, blocking collectives, attend(): shard_rows = lax.all_gather(keyval, 'seq', axis=0, tiled=True)  35.7 us
    reduce_scatter x1, waiting for transfers between devices, per_device(): lax.psum_scatter(second_update.astype(jnp.bfloat16), 'seq', scatter_dimen...  18.7 us
    psum x1, blocking collectives, per_device(): lax.psum(second_counts.astype(jnp.bfloat16), 'seq').astype(jnp.float32)  10.6 us
    dot_general x4, matrix products, recall(): numerator = jnp.dot(feature_rows, memory_state, precision=PRECISE)  9.52 us
  transfers between devices with their start and end apart: 6, of which 5 were waited for; matrix products, arithmetic and copies ran while one was open for 5% of the time, Pallas kernels for 0%

commit v1 on v0

--- a/solution.py
+++ b/solution.py
@@ -1,8 +1,12 @@
+import functools
 import math
 
 import jax
 import jax.numpy as jnp
+import numpy as np
 from jax import lax
+from jax.experimental import pallas as pl
+from jax.experimental.pallas import tpu as pltpu
 from jax.sharding import PartitionSpec as P
 
 HEAD_DIM = 128
@@ -152,9 +156,459 @@
     return (second_rows[None], (later_cols + final_share)[None], (later_norm + final_counts)[None])
 
 
+MESH = pl.DeviceIdType.MESH
+NN = (((1,), (0,)), ((), ()))
+NT = (((1,), (1,)), ((), ()))
+TN = (((0,), (0,)), ((), ()))
+(X_IN, P_IN, WOUT, FRESH, P_FRESH, KV, SQ, ATT, PK) = range(9)
+ROWS = 13
+N_KINDS = 14
+
+
+def mxu(left, right, dims, precision=None):
+    return lax.dot_general(
+        left, right, dims, precision=precision, preferred_element_type=jnp.float32
+    )
+
+
+def selection(key_dim):
+    width = 2 * key_dim
+    select = np.zeros((6 * width, key_dim), np.float32)
+    for number in range(3 * width):
+        offset, place = number // width + 1, number % width
+        for half, entry in ((0, place), (1, (place - offset) % width)):
+            select[half * 3 * width + number, entry % key_dim] = 1.0 if entry < key_dim else -1.0
+    return select
+
+
+def columns_kernel(
+    n,
+    n_phase,
+    rows_hbm,
+    fresh_hbm,
+    counts_ref,
+    memory_hbm,
+    norm_ref,
+    memq_hbm,
+    memk_hbm,
+    gain_ref,
+    wkv_hbm,
+    wout_hbm,
+    select_ref,
+    rows_out,
+    memory_out,
+    norm_out,
+    x1,
+    x2,
+    own_rows,
+    own_fresh,
+    memq,
+    memk,
+    wkv,
+    wout,
+    mem1,
+    mem2,
+    key_w,
+    query_w,
+    next_w,
+    p_in,
+    p_fresh,
+    p_second,
+    pq_out,
+    resid,
+    kv_out,
+    kv_in,
+    squares,
+    att,
+    pk,
+    out1,
+    out2,
+    send,
+    recv,
+    phase_send,
+    phase_recv,
+    local,
+):
+    me, ph = lax.axis_index("seq"), lax.axis_index("phase")
+    rows, cols = own_rows.shape[0], x1.shape[1]
+    width, depth = own_rows.shape[1], memq.shape[1]
+    kvw = wkv.shape[1] // 2
+    seg = n * rows
+    peers = [lax.rem(me + d, n) for d in range(n)]
+    origins = [lax.rem(me - d + n, n) for d in range(n)]
+    has_next, has_prev = ph < n_phase - 1, ph > 0
+
+    def columns(index):
+        return pl.ds(pl.multiple_of(index * cols, cols), cols)
+
+    def block(index):
+        return pl.ds(pl.multiple_of(index * rows, rows), rows)
+
+    def head(index, first=0):
+        return pl.ds(pl.multiple_of(first + index * HEAD_DIM, HEAD_DIM), HEAD_DIM)
+
+    def to_peer(kind, d, src, dst):
+        return pltpu.make_async_remote_copy(
+            src_ref=src,
+            dst_ref=dst,
+            send_sem=send.at[kind, d],
+            recv_sem=recv.at[kind, d],
+            device_id={"seq": peers[d]},
+            device_id_type=MESH,
+        )
+
+    def to_phase(kind, step, src, dst):
+        return pltpu.make_async_remote_copy(
+            src_ref=src,
+            dst_ref=dst,
+            send_sem=phase_send.at[kind],
+            recv_sem=phase_recv.at[kind],
+            device_id={"phase": ph + step},
+            device_id_type=MESH,
+        )
+
+    def here(number, src, dst):
+        return pltpu.make_async_copy(src, dst, local.at[number])
+
+    loads = [
+        here(0, rows_hbm.at[0], own_rows),
+        here(1, memq_hbm.at[0], memq),
+        here(2, memory_hbm.at[0], mem1),
+        here(3, rows_hbm.at[0, :, columns(me)], x1.at[block(me)]),
+        here(4, wkv_hbm.at[0], wkv),
+        here(5, memk_hbm.at[0], memk),
+        here(6, wout_hbm.at[0, :, columns(me)], wout.at[me]),
+        here(7, fresh_hbm, own_fresh),
+        here(8, fresh_hbm.at[:, columns(me)], x2.at[block(me)]),
+    ]
+    for copy in loads[:8]:
+        copy.start()
+
+    barrier = pltpu.get_barrier_semaphore()
+    for d in range(1, n):
+        pl.semaphore_signal(barrier, inc=1, device_id={"seq": peers[d]}, device_id_type=MESH)
+
+    @pl.when(has_next)
+    def _():
+        pl.semaphore_signal(barrier, inc=1, device_id={"phase": ph + 1}, device_id_type=MESH)
+
+    @pl.when(has_prev)
+    def _():
+        pl.semaphore_signal(barrier, inc=1, device_id={"phase": ph - 1}, device_id_type=MESH)
+
+    pl.semaphore_wait(barrier, n - 1 + has_next.astype(jnp.int32) + has_prev.astype(jnp.int32))
+
+    sent = []
+    x_copies = [
+        to_peer(X_IN, d, rows_hbm.at[0, :, columns(peers[d])], x1.at[block(me)])
+        for d in range(1, n)
+    ]
+    fresh_copies = [
+        to_peer(FRESH, d, fresh_hbm.at[:, columns(peers[d])], x2.at[block(me)])
+        for d in range(1, n)
+    ]
+    wout_copies = [
+        to_peer(WOUT, d, wout_hbm.at[0, :, columns(peers[d])], wout.at[me]) for d in range(1, n)
+    ]
+    p_copies = [to_peer(P_IN, d, p_in.at[me], p_in.at[me]) for d in range(1, n)]
+    pf_copies = [to_peer(P_FRESH, d, p_fresh.at[me], p_fresh.at[me]) for d in range(1, n)]
+    for copy in x_copies:
+        copy.start()
+    sent += x_copies + wout_copies + p_copies
+
+    line = lax.broadcasted_iota(jnp.int32, (depth, depth), 0)
+    unit = (line == lax.broadcasted_iota(jnp.int32, (depth, depth), 1)).astype(jnp.bfloat16)
+    loads[1].wait()
+    query_w[...] = mxu(unit, memq[...], NT).astype(jnp.bfloat16)
+    loads[0].wait()
+    p_in[me] = mxu(query_w[...], own_rows[...], NT)
+    for copy in p_copies:
+        copy.start()
+    weight_copy = to_phase(0, -1, query_w.at[:, columns(me)], next_w)
+
+    @pl.when(has_prev)
+    def _():
+        weight_copy.start()
+
+    loads[7].wait()
+
+    @pl.when(ph == 0)
+    def _():
+        loads[8].start()
+        p_fresh[me] = mxu(query_w[...], own_fresh[...], NT)
+        for copy in pf_copies + fresh_copies:
+            copy.start()
+
+    for copy in wout_copies:
+        copy.start()
+
+    loads[5].wait()
+    key_w[...] = mxu(unit, memk[...], NT).astype(jnp.bfloat16)
+
+    def across(projected):
+        pairs = mxu(select_ref[...], projected, NN, PRECISE)
+        pairs = jnp.maximum(pairs, 0.0)
+        half = pairs.shape[0] // 2
+        return pairs[:half] * pairs[half:]
+
+    def recalled(turned, mem_ref, norm_row):
+        upright = turned.T
+        scale = jnp.sum(upright * norm_row, axis=1, keepdims=True) + 1.0
+        found = mxu(upright.astype(jnp.bfloat16), mem_ref[...].astype(jnp.bfloat16), NN)
+        return found / scale, upright
+
+    def section(step, x_ref, projected, mem_ref, norm_row, valid, out_ref, after_output):
+        base = 4 * step
+        found, _ = recalled(across(projected), mem_ref, norm_row)
+        residual = x_ref[...].astype(jnp.float32) + found
+        resid[...] = residual
+        square = jnp.sum(residual * residual, axis=1, keepdims=True)
+        squares[step, me] = jnp.broadcast_to(square, (seg, 128)).T[:8]
+        copies = []
+        for d in range(1, n):
+            copy = to_peer(SQ + base, d, squares.at[step, me], squares.at[step, me])
+            copy.start()
+            copies.append(copy)
+        scaled = (residual * gain_ref[:, columns(me)]).astype(jnp.bfloat16)
+        if step == 0:
+            loads[4].wait()
+
+        def part(index):
+            keys = mxu(scaled, wkv[:, head(index)], NN)
+            values = mxu(scaled, wkv[:, head(index, kvw)], NN)
+            return jnp.concatenate([keys, values], axis=1)
+
+        for d in range(1, n):
+            kv_out[step, d] = part(peers[d]).astype(jnp.bfloat16)
+            copy = to_peer(KV + base, d, kv_out.at[step, d], kv_in.at[step, me])
+            copy.start()
+            copies.append(copy)
+        total = part(me)
+        sums = squares[step, me]
+        for copy in copies:
+            copy.wait_recv()
+        for d in range(1, n):
+            total = total + kv_in[step, origins[d]].astype(jnp.float32)
+            sums = sums + squares[step, origins[d]]
+        inverse = lax.rsqrt(sums[:1] / width + 1e-05)
+        inverse = jnp.broadcast_to(inverse, (128, seg)).T
+        keys = (total[:, :HEAD_DIM] * inverse).astype(jnp.bfloat16)
+        values = (total[:, HEAD_DIM:] * inverse).astype(jnp.bfloat16)
+        scores = mxu(keys, keys, NT) / math.sqrt(HEAD_DIM)
+        row_at = lax.broadcasted_iota(jnp.int32, (seg, seg), 0)
+        key_at = lax.broadcasted_iota(jnp.int32, (seg, seg), 1)
+        scores = jnp.where((key_at < valid) & (key_at != row_at), scores, -1e30)
+        weights = jnp.exp(scores - jnp.max(scores, axis=1, keepdims=True))
+        weight_sum = jnp.sum(weights, axis=1, keepdims=True)
+        attended = mxu(weights.astype(jnp.bfloat16), values, NN) / weight_sum
+        att[step, me] = attended.astype(jnp.bfloat16)
+        att_copies = []
+        for d in range(1, n):
+            copy = to_peer(ATT + base, d, att.at[step, me], att.at[step, me])
+            copy.start()
+            att_copies.append(copy)
+        if step == 0:
+            loads[6].wait()
+            for copy in wout_copies:
+                copy.wait_recv()
+        resid[...] += mxu(att[step, me], wout[me], NN)
+        for d in range(1, n):
+            att_copies[d - 1].wait_recv()
+            resid[...] += mxu(att[step, origins[d]], wout[origins[d]], NN)
+        output = resid[...].astype(jnp.bfloat16)
+        out_ref[...] = output
+        if step == 0:
+
+            @pl.when(has_next)
+            def _():
+                weight_in.wait_recv()
+
+            pk[step, me, pl.ds(depth, depth)] = mxu(next_w[...], output, NT)
+        pk[step, me, pl.ds(0, depth)] = mxu(key_w[:, columns(me)], output, NT)
+        taken = pl.ds(0, (2 - step) * depth)
+        pk_copies = []
+        for d in range(1, n):
+            copy = to_peer(PK + base, d, pk.at[step, me, taken], pk.at[step, me, taken])
+            copy.start()
+            pk_copies.append(copy)
+        after_output()
+        for copy in pk_copies:
+            copy.wait_recv()
+        projected = pk[step, 0, taken]
+        for index in range(1, n):
+            projected = projected + pk[step, index, taken]
+        if step == 0:
+            pq_out[...] = projected[depth:]
+
+            @pl.when(has_next)
+            def _():
+                pq_copy.start()
+
+        turned = across(projected[:depth])
+        found, upright = recalled(turned, mem_ref, norm_row)
+        live = (lax.broadcasted_iota(jnp.int32, (seg, 1), 0) < valid).astype(jnp.float32)
+        correction = (out_ref[...].astype(jnp.float32) - found) * live
+        update = mxu(turned.astype(jnp.bfloat16), correction.astype(jnp.bfloat16), NN)
+        counted = jnp.sum(upright * live, axis=0, keepdims=True)
+        sent.extend(copies + att_copies + pk_copies)
+        return update, counted
+
+    weight_in = to_phase(0, -1, query_w.at[:, columns(me)], next_w)
+    out_copy = to_phase(1, 1, out1, x2)
+    pq_copy = to_phase(2, 1, pq_out, p_second)
+
+    @pl.when(ph == n_phase - 1)
+    def _():
+        next_w[...] = jnp.zeros_like(next_w)
+
+    loads[2].wait()
+    loads[3].wait()
+    for copy in p_copies + x_copies:
+        copy.wait_recv()
+
+    def joined(ref):
+        return jnp.concatenate([ref[index] for index in range(n)], axis=1)
+
+    def pass_on():
+        @pl.when(has_next)
+        def _():
+            out_copy.start()
+
+    norm_row = norm_ref[...]
+    update, counted = section(
+        0, x1, joined(p_in), mem1, norm_row, counts_ref[ph + 1], out1, pass_on
+    )
+    mem2[...] = mem1[...] + update
+    norm_row = norm_row + counted
+
+    @pl.when(ph == 0)
+    def _():
+        for copy in pf_copies + fresh_copies:
+            copy.wait_recv()
+        loads[8].wait()
+        p_second[...] = joined(p_fresh)
+
+    @pl.when(has_prev)
+    def _():
+        pq_copy.wait_recv()
+        out_copy.wait_recv()
+
+    row_copies = []
+
+    def hand_out():
+        for d in range(1, n):
+            copy = to_peer(
+                ROWS, d, out2.at[block(peers[d])], rows_out.at[0, :, columns(me)]
+            )
+            copy.start()
+            row_copies.append(copy)
+        own_out.start()
+
+    own_out = here(9, out2.at[block(me)], rows_out.at[0, :, columns(me)])
+    update, counted = section(
+        1, x2, p_second[...], mem2, norm_row, counts_ref[ph], out2, hand_out
+    )
+    memory_out[0] = mem2[...] + update
+    norm_out[...] = norm_row + counted
+
+    own_out.wait()
+    for copy in row_copies:
+        copy.wait()
+    for copy in sent:
+        copy.wait_send()
+
+    @pl.when(ph == 0)
+    def _():
+        for copy in pf_copies + fresh_copies:
+            copy.wait_send()
+
+    @pl.when(has_prev)
+    def _():
+        weight_copy.wait_send()
+
+    @pl.when(has_next)
+    def _():
+        out_copy.wait_send()
+        pq_copy.wait_send()
+
+
+def by_columns(n, n_phase, *args):
+    phase_rows, memory, w_memq, w_kv, w_out = (args[0], args[3], args[5], args[8], args[9])
+    rows, width = phase_rows.shape[1:]
+    cols, depth, kv_cols = width // n, w_memq.shape[2], w_kv.shape[2]
+    states, seg = memory.shape[1], n * rows
+    half, full = jnp.bfloat16, jnp.float32
+    select = jnp.asarray(selection(depth))
+    any_space = pl.BlockSpec(memory_space=pl.ANY)
+    vmem = pl.BlockSpec(memory_space=pltpu.VMEM)
+    smem = pl.BlockSpec(memory_space=pltpu.SMEM)
+    scratch = [
+        ((seg, cols), half),
+        ((seg, cols), half),
+        ((rows, width), half),
+        ((rows, width), half),
+        ((width, depth), half),
+        ((width, depth), half),
+        ((cols, kv_cols), half),
+        ((n, HEAD_DIM, cols), half),
+        ((states, cols), full),
+        ((states, cols), full),
+        ((depth, width), half),
+        ((depth, width), half),
+        ((depth, cols), half),
+        ((n, depth, rows), full),
+        ((n, depth, rows), full),
+        ((depth, seg), full),
+        ((depth, seg), full),
+        ((seg, cols), full),
+        ((2, n, seg, 2 * HEAD_DIM), half),
+        ((2, n, seg, 2 * HEAD_DIM), half),
+        ((2, n, 8, seg), full),
+        ((2, n, seg, HEAD_DIM), half),
+        ((2, n, 2 * depth, seg), full),
+        ((seg, cols), half),
+        ((seg, cols), half),
+    ]
+    flops = 4 * seg * cols * (4 * states + kv_cols + n * HEAD_DIM)
+    return pl.pallas_call(
+        functools.partial(columns_kernel, n, n_phase),
+        out_shape=(
+            jax.ShapeDtypeStruct(phase_rows.shape, half),
+            jax.ShapeDtypeStruct(memory.shape, full),
+            jax.ShapeDtypeStruct(args[4].shape, full),
+        ),
+        in_specs=[any_space, any_space, smem, any_space, vmem]
+        + [any_space, any_space, vmem, any_space, any_space, vmem],
+        out_specs=(any_space, vmem, vmem),
+        scratch_shapes=[pltpu.VMEM(shape, kind) for shape, kind in scratch]
+        + [
+            pltpu.SemaphoreType.DMA((N_KINDS, n)),
+            pltpu.SemaphoreType.DMA((N_KINDS, n)),
+            pltpu.SemaphoreType.DMA((3,)),
+            pltpu.SemaphoreType.DMA((3,)),
+            pltpu.SemaphoreType.DMA((10,)),
+        ],
+        cost_estimate=pl.CostEstimate(
+            flops=flops, bytes_accessed=6_000_000, transcendentals=2 * seg * seg
+        ),
+        compiler_params=pltpu.CompilerParams(
+            collective_id=0, has_side_effects=True, vmem_limit_bytes=48 * 1024 * 1024
+        ),
+    )(*args, select)
+
+
+def dispatch(n, n_phase, *args):
+    rows, width = args[0].shape[1:]
+    heads = n * args[9].shape[1] // HEAD_DIM
+    fits = heads == n and width % (n * 128) == 0 and rows % 16 == 0 and (n * rows) % 128 == 0
+    if fits and n * rows <= 512:
+        return by_columns(n, n_phase, *args)
+    return per_device(*args)
+
+
 def solution(mesh):
     return jax.shard_map(
-        per_device,
+        functools.partial(dispatch, mesh.shape["seq"], mesh.shape["phase"]),
         mesh=mesh,
         in_specs=(
             P("phase", ("groups", "seq"), None),

time: 385 us -> 111 us (0.29)
  waiting for transfers between devices: 269 us -> 0 us
  Pallas kernels: 0 us -> 104 us
  blocking collectives: 55.7 us -> 0 us
  matrix products: 32.3 us -> 0 us
  between operations: 14.4 us -> 0.76 us
  other arithmetic: 8.66 us -> 0 us
  local copies, waits for them, and re-layouts: 0.82 us -> 6.79 us
    all_gather x3 -> x0, waiting for transfers between devices: 204 us -> none  [the longest x1 112 us: per_device(): lax.all_gather(w_kv[0], 'seq', axis=0, tiled=True)]
    pallas_call x0 -> x1, Pallas kernels: none -> 104 us  [by_columns(): pl.pallas_call(functools.partial(columns_kernel, n, n_phase), out_shape=(...]
    psum x1 -> x0, waiting for transfers between devices: 44.2 us -> none  [per_device(): lax.psum(first_update.astype(jnp.bfloat16), 'seq').astype(jnp.float32)]
    all_gather x2 -> x0, blocking collectives: 35.7 us -> none  [attend(): shard_rows = lax.all_gather(keyval, 'seq', axis=0, tiled=True)]
    dot_general x22 -> x0, matrix products: 32.3 us -> none  [the longest x4 9.52 us: recall(): numerator = jnp.dot(feature_rows, memory_state, precision=PRECISE)]
    psum x2 -> x0, blocking collectives: 20 us -> none  [the longest x1 10.6 us: per_device(): lax.psum(second_counts.astype(jnp.bfloat16), 'seq').astype(jnp.float32)]
    reduce_scatter x1 -> x0, waiting for transfers between devices: 18.7 us -> none  [per_device(): lax.psum_scatter(second_update.astype(jnp.bfloat16), 'seq', scatter_dimen...]
    unnamed x36 -> x21, local copies, waits for them, and re-layouts: 0.16 us -> 6.79 us
  transfers between devices with their start and end apart: 6 -> 0, of which waited for: 5 -> 0; matrix products, arithmetic and copies ran while one was open for 5% -> 0% of each run, Pallas kernels for 0% -> 0%
where the time goes in v1:
time: 111 us
  Pallas kernels  104 us (94%)
  local copies, waits for them, and re-layouts  6.79 us (6%)
    pallas_call x1, Pallas kernels, by_columns(): pl.pallas_call(functools.partial(columns_kernel, n, n_phase), out_shape=(...  104 us
    unnamed x21, local copies, waits for them, and re-layouts  6.79 us

profile of v1, /device:TPU:0, one launch (start us, length us, event | category | flops | bytes accessed | tf_op | source)
XLA Modules:
  0.0 111.3 jit_solution(10323654219625299386)
XLA Ops:
  0.6 0.0 copy-start
  0.6 0.0 copy-start.4
  0.7 0.0 copy-start.5
  0.7 0.0 copy-start.1
  0.7 0.0 copy-start.6
  0.7 0.0 copy-start.2
  0.7 1.4 %copy.14.memq_hbm = bf16[1,3072,32]{2,1,0:T(8,128)(2,1)S(1)} copy(bf16[1,3072,32]{1,2,0:T(8,128)(2,1)} %param.16) | data formatting | bytes 393216 | tf_op args[5]
  2.1 1.3 %copy.15.memk_hbm = bf16[1,3072,32]{2,1,0:T(8,128)(2,1)S(1)} copy(bf16[1,3072,32]{1,2,0:T(8,128)(2,1)} %param.17) | data formatting | bytes 393216 | tf_op args[6]
  3.4 0.0 copy-done
  3.4 0.0 copy-done.4
  3.4 0.0 copy-done.5
  3.5 0.0 copy-done.1
  3.5 0.0 copy-done.6
  3.5 0.0 copy-done.2
  3.5 0.0 copy-start.3
  3.5 1.0 copy-done.3
  4.5 0.0 copy-start.7
  4.5 0.9 copy-done.7
  5.4 103.7 %shard_map.130 = (bf16[1,64,3072]{2,1,0:T(8,128)(2,1)S(1)}, f32[1,192,768]{2,1,0:T(8,128)S(1)}, f32[1,192]{1,0:T(1,128)S(1)}) custom-call(bf16[1,64,3072]{2,1,0:T(8,128)(2,1)S(1)} %copy-done.2, bf16[64,3072]{1,0:T(8,128)(2,1)S(1)} %copy-done.3, s32[5]{0:T(128)S(1)} %copy-done.6, f32[1,192,768]{2,1,0:T(8,128)S(1)} %copy-done.1, f32[1,192]{1,0:T(1,128)S(1)} %copy-done.5, ...), custom_call_target="tpu_custom_call" | custom-call | flops 1811939328 | bytes 6000000 | tf_op jit(solution)/shard_map/pallas_call | solution.py:573
  109.1 0.7 copy.19
  109.9 0.8 copy.20
  110.7 0.6 copy.21
Async XLA Ops:
  0.6 2.8 %copy-start = (bf16[1,128,3072]{2,1,0:T(8,128)(2,1)S(1)}, bf16[1,128,3072]{2,1,0:T(8,128)(2,1)}, u32[]{:S(2)}) copy-start(bf16[1,128,3072]{2,1,0:T(8,128)(2,1)} %wout_hbm.1) | copy-start | bytes 2359300
  0.6 2.8 %copy-start.4 = (f32[1,3072]{1,0:T(1,128)S(1)}, f32[1,3072]{1,0:T(1,128)}, u32[]{:S(2)}) copy-start(f32[1,3072]{1,0:T(1,128)} %gain_ref.1) | copy-start | bytes 36868
  0.7 2.8 %copy-start.5 = (f32[1,192]{1,0:T(1,128)S(1)}, f32[1,192]{1,0:T(1,128)}, u32[]{:S(2)}) copy-start(f32[1,192]{1,0:T(1,128)} %norm_ref.1) | copy-start | bytes 2308
  0.7 2.8 %copy-start.1 = (f32[1,192,768]{2,1,0:T(8,128)S(1)}, f32[1,192,768]{2,1,0:T(8,128)}, u32[]{:S(2)}) copy-start(f32[1,192,768]{2,1,0:T(8,128)} %memory_hbm.1) | copy-start | bytes 1769476
  0.7 2.8 %copy-start.6 = (s32[5]{0:T(128)S(1)}, s32[5]{0:T(128)}, u32[]{:S(2)}) copy-start(s32[5]{0:T(128)} %counts_ref.1) | copy-start | bytes 64
  0.7 2.8 %copy-start.2 = (bf16[1,64,3072]{2,1,0:T(8,128)(2,1)S(1)}, bf16[1,64,3072]{2,1,0:T(8,128)(2,1)}, u32[]{:S(2)}) copy-start(bf16[1,64,3072]{2,1,0:T(8,128)(2,1)} %rows_hbm.1) | copy-start | bytes 1179652
  3.5 1.0 copy-start.3
  4.5 0.9 copy-start.7

commit v2 on v1

--- a/solution.py
+++ b/solution.py
@@ -3,7 +3,6 @@
 
 import jax
 import jax.numpy as jnp
-import numpy as np
 from jax import lax
 from jax.experimental import pallas as pl
 from jax.experimental.pallas import tpu as pltpu
@@ -173,12 +172,17 @@
 
 def selection(key_dim):
     width = 2 * key_dim
-    select = np.zeros((6 * width, key_dim), np.float32)
-    for number in range(3 * width):
-        offset, place = number // width + 1, number % width
-        for half, entry in ((0, place), (1, (place - offset) % width)):
-            select[half * 3 * width + number, entry % key_dim] = 1.0 if entry < key_dim else -1.0
-    return select
+    shape = (6 * width, key_dim)
+    number = lax.broadcasted_iota(jnp.int32, shape, 0)
+    source = lax.broadcasted_iota(jnp.int32, shape, 1)
+    second = number >= 3 * width
+    within = jnp.where(second, number - 3 * width, number)
+    offset = 1 + (within >= width).astype(jnp.int32) + (within >= 2 * width).astype(jnp.int32)
+    place = within - (offset - 1) * width
+    turned = place - offset
+    turned = jnp.where(turned < 0, turned + width, turned)
+    entry = jnp.where(second, turned, place)
+    return (entry == source).astype(jnp.float32) - (entry == source + key_dim).astype(jnp.float32)
 
 
 def columns_kernel(
@@ -189,12 +193,11 @@
     counts_ref,
     memory_hbm,
     norm_ref,
-    memq_hbm,
-    memk_hbm,
+    query_w,
+    key_w,
     gain_ref,
     wkv_hbm,
     wout_hbm,
-    select_ref,
     rows_out,
     memory_out,
     norm_out,
@@ -202,14 +205,10 @@
     x2,
     own_rows,
     own_fresh,
-    memq,
-    memk,
     wkv,
     wout,
     mem1,
     mem2,
-    key_w,
-    query_w,
     next_w,
     p_in,
     p_fresh,
@@ -227,11 +226,13 @@
     recv,
     phase_send,
     phase_recv,
+    group_send,
+    group_recv,
     local,
 ):
     me, ph = lax.axis_index("seq"), lax.axis_index("phase")
     rows, cols = own_rows.shape[0], x1.shape[1]
-    width, depth = own_rows.shape[1], memq.shape[1]
+    width, depth = own_rows.shape[1], next_w.shape[0]
     kvw = wkv.shape[1] // 2
     seg = n * rows
     peers = [lax.rem(me + d, n) for d in range(n)]
@@ -270,18 +271,14 @@
     def here(number, src, dst):
         return pltpu.make_async_copy(src, dst, local.at[number])
 
-    loads = [
-        here(0, rows_hbm.at[0], own_rows),
-        here(1, memq_hbm.at[0], memq),
-        here(2, memory_hbm.at[0], mem1),
-        here(3, rows_hbm.at[0, :, columns(me)], x1.at[block(me)]),
-        here(4, wkv_hbm.at[0], wkv),
-        here(5, memk_hbm.at[0], memk),
-        here(6, wout_hbm.at[0, :, columns(me)], wout.at[me]),
-        here(7, fresh_hbm, own_fresh),
-        here(8, fresh_hbm.at[:, columns(me)], x2.at[block(me)]),
-    ]
-    for copy in loads[:8]:
+    own_load = here(0, rows_hbm.at[0], own_rows)
+    memory_load = here(1, memory_hbm.at[0], mem1)
+    x_load = here(2, rows_hbm.at[0, :, columns(me)], x1.at[block(me)])
+    kv_load = here(3, wkv_hbm.at[0], wkv)
+    wout_load = here(4, wout_hbm.at[0, :, columns(me)], wout.at[me])
+    own_fresh_load = here(5, fresh_hbm, own_fresh)
+    fresh_load = here(6, fresh_hbm.at[:, columns(me)], x2.at[block(me)])
+    for copy in (own_load, x_load, own_fresh_load, memory_load, kv_load, wout_load):
         copy.start()
 
     barrier = pltpu.get_barrier_semaphore()
@@ -296,9 +293,13 @@
     def _():
         pl.semaphore_signal(barrier, inc=1, device_id={"phase": ph - 1}, device_id_type=MESH)
 
-    pl.semaphore_wait(barrier, n - 1 + has_next.astype(jnp.int32) + has_prev.astype(jnp.int32))
+    other = 1 - lax.axis_index("groups")
+    pl.semaphore_signal(barrier, inc=1, device_id={"groups": other}, device_id_type=MESH)
+    pl.semaphore_wait(barrier, n + has_next.astype(jnp.int32) + has_prev.astype(jnp.int32))
 
     sent = []
+    half_rows = wout.shape[1] // 2
+    half = pl.ds(pl.multiple_of((1 - other) * half_rows, half_rows), half_rows)
     x_copies = [
         to_peer(X_IN, d, rows_hbm.at[0, :, columns(peers[d])], x1.at[block(me)])
         for d in range(1, n)
@@ -308,45 +309,52 @@
         for d in range(1, n)
     ]
     wout_copies = [
-        to_peer(WOUT, d, wout_hbm.at[0, :, columns(peers[d])], wout.at[me]) for d in range(1, n)
+        to_peer(WOUT, d, wout_hbm.at[0, half, columns(peers[d])], wout.at[me, half])
+        for d in range(1, n)
+    ]
+    across_copies = [
+        pltpu.make_async_remote_copy(
+            src_ref=wout.at[origins[d], half],
+            dst_ref=wout.at[origins[d], half],
+            send_sem=group_send.at[d],
+            recv_sem=group_recv.at[d],
+            device_id={"groups": other},
+            device_id_type=MESH,
+        )
+        for d in range(1, n)
     ]
     p_copies = [to_peer(P_IN, d, p_in.at[me], p_in.at[me]) for d in range(1, n)]
     pf_copies = [to_peer(P_FRESH, d, p_fresh.at[me], p_fresh.at[me]) for d in range(1, n)]
     for copy in x_copies:
         copy.start()
-    sent += x_copies + wout_copies + p_copies
-
-    line = lax.broadcasted_iota(jnp.int32, (depth, depth), 0)
-    unit = (line == lax.broadcasted_iota(jnp.int32, (depth, depth), 1)).astype(jnp.bfloat16)
-    loads[1].wait()
-    query_w[...] = mxu(unit, memq[...], NT).astype(jnp.bfloat16)
-    loads[0].wait()
-    p_in[me] = mxu(query_w[...], own_rows[...], NT)
+    sent += x_copies + wout_copies + across_copies + p_copies
+
+    own_load.wait()
+    p_in[me] = mxu(query_w[0], own_rows[...], NT)
     for copy in p_copies:
         copy.start()
-    weight_copy = to_phase(0, -1, query_w.at[:, columns(me)], next_w)
+    weight_copy = to_phase(0, -1, query_w.at[0, :, columns(me)], next_w)
 
     @pl.when(has_prev)
     def _():
         weight_copy.start()
 
-    loads[7].wait()
+    own_fresh_load.wait()
 
     @pl.when(ph == 0)
     def _():
-        loads[8].start()
-        p_fresh[me] = mxu(query_w[...], own_fresh[...], NT)
-        for copy in pf_copies + fresh_copies:
+        fresh_load.start()
+        p_fresh[me] = mxu(query_w[0], own_fresh[...], NT)
+        for copy in pf_copies:
             copy.start()
 
     for copy in wout_copies:
         copy.start()
 
-    loads[5].wait()
-    key_w[...] = mxu(unit, memk[...], NT).astype(jnp.bfloat16)
+    select = selection(depth)
 
     def across(projected):
-        pairs = mxu(select_ref[...], projected, NN, PRECISE)
+        pairs = mxu(select, projected, NN, PRECISE)
         pairs = jnp.maximum(pairs, 0.0)
         half = pairs.shape[0] // 2
         return pairs[:half] * pairs[half:]
@@ -371,7 +379,7 @@
             copies.append(copy)
         scaled = (residual * gain_ref[:, columns(me)]).astype(jnp.bfloat16)
         if step == 0:
-            loads[4].wait()
+            kv_load.wait()
 
         def part(index):
             keys = mxu(scaled, wkv[:, head(index)], NN)
@@ -384,6 +392,10 @@
             copy.start()
             copies.append(copy)
         total = part(me)
+        if step == 0:
+            for copy, relay in zip(wout_copies, across_copies):
+                copy.wait_recv()
+                relay.start()
         sums = squares[step, me]
         for copy in copies:
             copy.wait_recv()
@@ -408,8 +420,8 @@
             copy.start()
             att_copies.append(copy)
         if step == 0:
-            loads[6].wait()
-            for copy in wout_copies:
+            wout_load.wait()
+            for copy in across_copies:
                 copy.wait_recv()
         resid[...] += mxu(att[step, me], wout[me], NN)
         for d in range(1, n):
@@ -424,7 +436,7 @@
                 weight_in.wait_recv()
 
             pk[step, me, pl.ds(depth, depth)] = mxu(next_w[...], output, NT)
-        pk[step, me, pl.ds(0, depth)] = mxu(key_w[:, columns(me)], output, NT)
+        pk[step, me, pl.ds(0, depth)] = mxu(key_w[0, :, columns(me)], output, NT)
         taken = pl.ds(0, (2 - step) * depth)
         pk_copies = []
         for d in range(1, n):
@@ -453,7 +465,7 @@
         sent.extend(copies + att_copies + pk_copies)
         return update, counted
 
-    weight_in = to_phase(0, -1, query_w.at[:, columns(me)], next_w)
+    weight_in = to_phase(0, -1, query_w.at[0, :, columns(me)], next_w)
     out_copy = to_phase(1, 1, out1, x2)
     pq_copy = to_phase(2, 1, pq_out, p_second)
 
@@ -461,8 +473,8 @@
     def _():
         next_w[...] = jnp.zeros_like(next_w)
 
-    loads[2].wait()
-    loads[3].wait()
+    memory_load.wait()
+    x_load.wait()
     for copy in p_copies + x_copies:
         copy.wait_recv()
 
@@ -474,6 +486,11 @@
         def _():
             out_copy.start()
 
+        @pl.when(ph == 0)
+        def _():
+            for copy in fresh_copies:
+                copy.start()
+
     norm_row = norm_ref[...]
     update, counted = section(
         0, x1, joined(p_in), mem1, norm_row, counts_ref[ph + 1], out1, pass_on
@@ -485,7 +502,7 @@
     def _():
         for copy in pf_copies + fresh_copies:
             copy.wait_recv()
-        loads[8].wait()
+        fresh_load.wait()
         p_second[...] = joined(p_fresh)
 
     @pl.when(has_prev)
@@ -504,7 +521,7 @@
             row_copies.append(copy)
         own_out.start()
 
-    own_out = here(9, out2.at[block(me)], rows_out.at[0, :, columns(me)])
+    own_out = here(7, out2.at[block(me)], rows_out.at[0, :, columns(me)])
     update, counted = section(
         1, x2, p_second[...], mem2, norm_row, counts_ref[ph], out2, hand_out
     )
@@ -538,8 +555,9 @@
     cols, depth, kv_cols = width // n, w_memq.shape[2], w_kv.shape[2]
     states, seg = memory.shape[1], n * rows
     half, full = jnp.bfloat16, jnp.float32
-    select = jnp.asarray(selection(depth))
-    any_space = pl.BlockSpec(memory_space=pl.ANY)
+    w_memk = args[6]
+    args = args[:5] + (jnp.swapaxes(w_memq, 1, 2), jnp.swapaxes(w_memk, 1, 2)) + args[7:]
+    any_space = pl.BlockSpec(memory_space=pltpu.HBM)
     vmem = pl.BlockSpec(memory_space=pltpu.VMEM)
     smem = pl.BlockSpec(memory_space=pltpu.SMEM)
     scratch = [
@@ -547,14 +565,10 @@
         ((seg, cols), half),
         ((rows, width), half),
         ((rows, width), half),
-        ((width, depth), half),
-        ((width, depth), half),
         ((cols, kv_cols), half),
         ((n, HEAD_DIM, cols), half),
         ((states, cols), full),
         ((states, cols), full),
-        ((depth, width), half),
-        ((depth, width), half),
         ((depth, cols), half),
         ((n, depth, rows), full),
         ((n, depth, rows), full),
@@ -578,7 +592,7 @@
             jax.ShapeDtypeStruct(args[4].shape, full),
         ),
         in_specs=[any_space, any_space, smem, any_space, vmem]
-        + [any_space, any_space, vmem, any_space, any_space, vmem],
+        + [vmem, vmem, vmem, any_space, any_space],
         out_specs=(any_space, vmem, vmem),
         scratch_shapes=[pltpu.VMEM(shape, kind) for shape, kind in scratch]
         + [
@@ -586,29 +600,31 @@
             pltpu.SemaphoreType.DMA((N_KINDS, n)),
             pltpu.SemaphoreType.DMA((3,)),
             pltpu.SemaphoreType.DMA((3,)),
-            pltpu.SemaphoreType.DMA((10,)),
+            pltpu.SemaphoreType.DMA((n,)),
+            pltpu.SemaphoreType.DMA((n,)),
+            pltpu.SemaphoreType.DMA((8,)),
         ],
         cost_estimate=pl.CostEstimate(
             flops=flops, bytes_accessed=6_000_000, transcendentals=2 * seg * seg
         ),
         compiler_params=pltpu.CompilerParams(
-            collective_id=0, has_side_effects=True, vmem_limit_bytes=48 * 1024 * 1024
+            collective_id=0, has_side_effects=True, vmem_limit_bytes=60 * 1024 * 1024
         ),
-    )(*args, select)
-
-
-def dispatch(n, n_phase, *args):
+    )(*args)
+
+
+def dispatch(n, n_phase, n_groups, *args):
     rows, width = args[0].shape[1:]
     heads = n * args[9].shape[1] // HEAD_DIM
     fits = heads == n and width % (n * 128) == 0 and rows % 16 == 0 and (n * rows) % 128 == 0
-    if fits and n * rows <= 512:
+    if fits and n_groups == 2 and n * rows <= 512:
         return by_columns(n, n_phase, *args)
     return per_device(*args)
 
 
 def solution(mesh):
     return jax.shard_map(
-        functools.partial(dispatch, mesh.shape["seq"], mesh.shape["phase"]),
+        functools.partial(dispatch, mesh.shape["seq"], mesh.shape["phase"], mesh.shape["groups"]),
         mesh=mesh,
         in_specs=(
             P("phase", ("groups", "seq"), None),

time: 111 us -> 93.6 us (0.84)
  Pallas kernels: 104 us -> 88.5 us
  local copies, waits for them, and re-layouts: 6.79 us -> 4.25 us
    pallas_call x1, Pallas kernels: 104 us -> 88.5 us  [by_columns(): pl.pallas_call(functools.partial(columns_kernel, n, n_phase), out_shape=(...]
    unnamed x21 -> x5, local copies, waits for them, and re-layouts: 6.79 us -> 4.25 us
where the time goes in v2:
time: 93.6 us; the launch traced here: 93.4 us
  Pallas kernels  88.5 us (95%)
  local copies, waits for them, and re-layouts  4.25 us (5%)
    pallas_call x1, Pallas kernels, by_columns(): pl.pallas_call(functools.partial(columns_kernel, n, n_phase), out_shape=(...  88.5 us
    unnamed x5, local copies, waits for them, and re-layouts  4.25 us

profile of v2, /device:TPU:0, one launch (start us, length us, event | category | flops | bytes accessed | tf_op | source)
XLA Modules:
  0.0 93.4 jit_solution(12429121212381177486)
XLA Ops:
  0.6 88.5 %shard_map.121 = (bf16[1,64,3072]{2,1,0:T(8,128)(2,1)}, f32[1,192,768]{2,1,0:T(8,128)}, f32[1,192]{1,0:T(1,128)}) custom-call(bf16[1,64,3072]{2,1,0:T(8,128)(2,1)} %rows_hbm.1, bf16[64,3072]{1,0:T(8,128)(2,1)} %fresh_hbm.1, s32[5]{0:T(128)} %counts_ref.1, f32[1,192,768]{2,1,0:T(8,128)} %memory_hbm.1, f32[1,192]{1,0:T(1,128)} %norm_ref.1, ...), custom_call_target="tpu_custom_call" | custom-call | flops 1811939328 | bytes 6000000 | tf_op jit(solution)/shard_map/pallas_call | solution.py:587
  89.2 0.0 copy-start
  89.2 1.8 %copy.16 = bf16[1,64,3072]{2,1,0:T(8,128)(2,1)} copy(bf16[1,64,3072]{2,1,0:T(8,128)(2,1)} %get-tuple-element.6) | data formatting | bytes 786432
  91.0 1.9 %copy.17 = f32[1,192,768]{2,1,0:T(8,128)} copy(f32[1,192,768]{2,1,0:T(8,128)} %get-tuple-element.7) | data formatting | bytes 1179648
  92.9 0.0 copy-done
  92.9 0.6 copy.18
Async XLA Ops:
  89.2 3.7 %copy-start = (f32[1,192]{1,0:T(1,128)S(1)}, f32[1,192]{1,0:T(1,128)}, u32[]{:S(2)}) copy-start(f32[1,192]{1,0:T(1,128)} %get-tuple-element.8) | copy-start | bytes 2308

commit v3 on v2

--- a/solution.py
+++ b/solution.py
@@ -435,8 +435,8 @@
             def _():
                 weight_in.wait_recv()
 
-            pk[step, me, pl.ds(depth, depth)] = mxu(next_w[...], output, NT)
-        pk[step, me, pl.ds(0, depth)] = mxu(key_w[0, :, columns(me)], output, NT)
+            pk[step, me, pl.ds(depth, depth)] = mxu(next_w[...], output, NT).astype(jnp.bfloat16)
+        pk[step, me, pl.ds(0, depth)] = mxu(key_w[0, :, columns(me)], output, NT).astype(jnp.bfloat16)
         taken = pl.ds(0, (2 - step) * depth)
         pk_copies = []
         for d in range(1, n):
@@ -446,9 +446,9 @@
         after_output()
         for copy in pk_copies:
             copy.wait_recv()
-        projected = pk[step, 0, taken]
+        projected = pk[step, 0, taken].astype(jnp.float32)
         for index in range(1, n):
-            projected = projected + pk[step, index, taken]
+            projected = projected + pk[step, index, taken].astype(jnp.float32)
         if step == 0:
             pq_out[...] = projected[depth:]
 
@@ -579,7 +579,7 @@
         ((2, n, seg, 2 * HEAD_DIM), half),
         ((2, n, 8, seg), full),
         ((2, n, seg, HEAD_DIM), half),
-        ((2, n, 2 * depth, seg), full),
+        ((2, n, 2 * depth, seg), half),
         ((seg, cols), half),
         ((seg, cols), half),
     ]

time: 93.6 us -> 91.4 us (0.976)
  Pallas kernels: 88.5 us -> 86.3 us
    pallas_call x1, Pallas kernels: 88.5 us -> 86.3 us  [by_columns(): pl.pallas_call(functools.partial(columns_kernel, n, n_phase), out_shape=(...]
where the time goes in v3:
time: 91.4 us; the launch traced here: 91.2 us
  Pallas kernels  86.3 us (94%)
  local copies, waits for them, and re-layouts  4.25 us (5%)
    pallas_call x1, Pallas kernels, by_columns(): pl.pallas_call(functools.partial(columns_kernel, n, n_phase), out_shape=(...  86.3 us
    unnamed x5, local copies, waits for them, and re-layouts  4.25 us

profile of v3, /device:TPU:0, one launch (start us, length us, event | category | flops | bytes accessed | tf_op | source)
XLA Modules:
  0.0 91.2 jit_solution(12047792528783996267)
XLA Ops:
  0.6 86.3 %shard_map.121 = (bf16[1,64,3072]{2,1,0:T(8,128)(2,1)}, f32[1,192,768]{2,1,0:T(8,128)}, f32[1,192]{1,0:T(1,128)}) custom-call(bf16[1,64,3072]{2,1,0:T(8,128)(2,1)} %rows_hbm.1, bf16[64,3072]{1,0:T(8,128)(2,1)} %fresh_hbm.1, s32[5]{0:T(128)} %counts_ref.1, f32[1,192,768]{2,1,0:T(8,128)} %memory_hbm.1, f32[1,192]{1,0:T(1,128)} %norm_ref.1, ...), custom_call_target="tpu_custom_call" | custom-call | flops 1811939328 | bytes 6000000 | tf_op jit(solution)/shard_map/pallas_call | solution.py:587
  86.9 0.0 copy-start
  87.0 1.8 %copy.16 = bf16[1,64,3072]{2,1,0:T(8,128)(2,1)} copy(bf16[1,64,3072]{2,1,0:T(8,128)(2,1)} %get-tuple-element.6) | data formatting | bytes 786432
  88.7 1.9 %copy.17 = f32[1,192,768]{2,1,0:T(8,128)} copy(f32[1,192,768]{2,1,0:T(8,128)} %get-tuple-element.7) | data formatting | bytes 1179648
  90.6 0.0 copy-done
  90.6 0.6 copy.18
Async XLA Ops:
  86.9 3.7 %copy-start = (f32[1,192]{1,0:T(1,128)S(1)}, f32[1,192]{1,0:T(1,128)}, u32[]{:S(2)}) copy-start(f32[1,192]{1,0:T(1,128)} %get-tuple-element.8) | copy-start | bytes 2308
